TPU v7x, 32 devices: a whole 2x2x4 slice. The times are simulated.
32 devices in a mesh: inlet: 4 (over y, x), row: 8 (over z, core).
Axes of the slice: x: 2, y: 2, z: 4, core: 2. Of those that a mesh axis runs over, the one named last changes fastest.
Arguments:
- coeffs: float32 [4, 1024, 1024], P('inlet', 'row'), may hold values from -6 to 6
- basis: float32 [4, 2048, 3, 1024], P('inlet', 'row'), may hold values from -0.1875 to 0.1875
- route: int32 [8192, 1], P(('inlet', 'row')), may hold values from 0 to 31; in each aligned block of 256 rows (0 to 255, 256 to 511, ...) at most 12 rows name the same one
Outputs:
- inflow: bfloat16 [12288, 3, 1024], P(('inlet', 'row'))
Inputs may be any that keep to these rules, and one draw needn't show every extreme that they name: `route`: among the rows of one device, no owner is named more than 12 times, a bound that some block reaches.
All inputs are finite; a program needn't handle non-finite values.
Results may differ from a plain program's by a relative error of at most 0.001.
Values may be sent and summed in bfloat16 or wider, within the bound.
A program may use at most 64 MiB of HBM per device.

v0:
```python
import jax
import jax.numpy as jnp
from jax import lax
from jax.sharding import PartitionSpec as P


def local(coeffs, basis, route):
    local_basis = basis[0]
    points = local_basis.shape[0]
    steps_total = coeffs.shape[1] * lax.axis_size("row")
    velocity = jnp.einsum(
        "pcm,tm->pct",
        local_basis,
        lax.all_gather(coeffs, "row", axis=1, tiled=True)[0],
        precision=lax.Precision.HIGHEST,
    )
    velocity = velocity.astype(jnp.bfloat16).reshape(points, 3 * steps_total)
    count = lax.axis_size(("inlet", "row"))
    capacity = 3 * points // (2 * count)
    owner = route[:, 0]
    onehot = (owner[:, None] == jnp.arange(count, dtype=jnp.int32)[None, :]).astype(jnp.int32)
    running = jnp.cumsum(onehot, axis=0)
    rank = jnp.sum(onehot * running, axis=1) - 1
    slot = owner * capacity + rank
    packed = jnp.zeros((count * capacity, 3 * steps_total), jnp.bfloat16).at[slot].set(velocity)
    moved = lax.all_to_all(
        packed.reshape(count, capacity, 3 * steps_total),
        ("inlet", "row"),
        split_axis=0,
        concat_axis=0,
        tiled=True,
    )
    return moved.reshape(count * capacity, 3, steps_total)


def solution(mesh):
    in_specs = (P("inlet", "row", None), P("inlet", "row", None, None), P(("inlet", "row"), None))
    out_specs = P(("inlet", "row"), None, None)
    return jax.shard_map(local, mesh=mesh, in_specs=in_specs, out_specs=out_specs, check_vma=False)
```

profile of v0, /device:TPU:0, one launch (start us, length us, event | category | flops | bytes accessed | tf_op | source)
XLA Modules:
  0.0 181.0 jit_solution(9071549521958825289)
XLA Ops:
  6.5 0.0 copy-start
  6.5 0.0 all-gather.2.cloned.1.call-start
  6.5 0.7 all-gather.2.cloned.1.call-update
  7.3 0.9 fusion.12
  8.2 0.6 reduce-window.6
  8.7 0.2 slice_reduce_fusion
  9.0 0.8 fusion.11
  9.8 0.7 compare_select_fusion
  10.4 48.4 %all-gather.2.cloned.1.call-done = f32[1,1024,1024]{2,1,0:T(8,128)} async-done(((f32[1,128,1024]{2,1,0:T(8,128)}), f32[1,1024,1024]{2,1,0:T(8,128)}) %all-gather.2.cloned.1.call-update) | async-done | bytes 4194320 | tf_op jit(solution)/shard_map/all_gather | solution.py:14
  58.8 0.0 copy-done
  58.8 12.7 %fusion.3 = bf16[256,3,1024]{2,0,1:T(8,128)(2,1)} fusion(f32[1,1024,1024]{2,1,0:T(8,128)} %all-gather.2.cloned.1.call-done, f32[1,256,3,1024]{3,1,2,0:T(8,128)S(1)} %copy-done), kind=kOutput, calls=%fused_computation.4 | convolution fusion | flops 9664462848 | bytes 8912896 | tf_op jit(solution)/shard_map/pcm,tm->pct/dot_general | solution.py:11
  71.5 2.6 %copy.8 = bf16[256,3,1024]{0,2,1:T(8,128)(2,1)} copy(bf16[256,3,1024]{2,0,1:T(8,128)(2,1)} %fusion.3) | data formatting | bytes 3145728 | tf_op jit(solution)/shard_map/convert_element_type | solution.py:17
  74.1 2.6 %copy.9 = bf16[256,3072]{1,0:T(8,128)(2,1)} copy(bf16[256,3072]{0,1:T(8,128)(2,1)} %bitcast.32) | data formatting | bytes 3145728 | tf_op jit(solution)/shard_map/reshape | solution.py:17
  76.7 5.3 %scatter_custom_fusion = bf16[384,3072]{1,0:T(8,128)(2,1)} fusion(s32[256]{0:T(256)S(1)} %bitcast.36, bf16[256,3072]{1,0:T(8,128)(2,1)} %copy.9, bf16[]{:T(256)} %constant.5.clone.1), kind=kCustom, calls=%fused_computation.5 | custom fusion | bytes 2359808 | tf_op jit(solution)/shard_map/scatter | solution.py:25
  82.0 4.3 %reshape.36 = bf16[32,12,3072]{2,1,0:T(8,128)(2,1)} reshape(bf16[384,3072]{1,0:T(8,128)(2,1)} %scatter_custom_fusion) | data formatting | bytes 4718592 | tf_op jit(solution)/shard_map/reshape | solution.py:27
  86.3 76.0 %all_to_all.5 = bf16[32,12,3072]{2,1,0:T(8,128)(2,1)} all-to-all(bf16[32,12,3072]{2,1,0:T(8,128)(2,1)} %reshape.36), channel_id=1, replica_groups=mesh['inlet'=4,'row'=8] {'inlet','row'}, dimensions={0} | all-to-all | bytes 4718592 | tf_op jit(solution)/shard_map/all_to_all | solution.py:26
  162.3 7.6 %reshape.37 = bf16[384,3,1024]{2,1,0:T(4,128)(2,1)} reshape(bf16[32,12,3072]{2,1,0:T(8,128)(2,1)} %all_to_all.5) | data formatting | bytes 4718592 | tf_op jit(solution)/shard_map/reshape | solution.py:33
  170.0 4.2 %copy.10 = bf16[384,3,1024]{2,0,1:T(8,128)(2,1)} copy(bf16[384,3,1024]{2,1,0:T(4,128)(2,1)} %reshape.37) | data formatting | bytes 4718592 | tf_op jit(solution)/shard_map/reshape | solution.py:33
  (3 shorter events, 0.0 us)
Async XLA Ops:
  6.5 52.3 %copy-start = (f32[1,256,3,1024]{3,1,2,0:T(8,128)S(1)}, f32[1,256,3,1024]{3,1,2,0:T(8,128)}, u32[]{:S(2)}) copy-start(f32[1,256,3,1024]{3,1,2,0:T(8,128)} %param.4) | copy-start | bytes 9437188
  6.5 52.3 %all-gather.2.cloned.1.call-start = ((), (), s32[]{:S(2)}) async-start(), calls=%async_computation.1 | async-start | bytes 4718592 | tf_op jit(solution)/shard_map/all_gather | solution.py:14
Sparse Core Ops, SparseCore 0:
  9.0 49.8 all-gather.1
where the time goes:
time: 182 us; the launch traced here: 181 us
  blocking collectives  76 us (42%)
  waiting for transfers between devices  49.1 us (27%)
  local copies, waits for them, and re-layouts  26.8 us (15%)
  between operations  13.4 us (7%)
  matrix products  12.7 us (7%)
  other arithmetic  2.99 us (2%)
    all_to_all x1, blocking collectives, local(): lax.all_to_all(packed.reshape(count, capacity, 3 * steps_total), ('inlet'...  76 us
    all_gather x1, waiting for transfers between devices, local(): lax.all_gather(coeffs, 'row', axis=1, tiled=True)[0]  48.4 us
    dot_general x1, matrix products, local(): jnp.einsum('pcm,tm->pct', local_basis, lax.all_gather(coeffs, 'row', axis...  12.7 us
    reshape x2, local copies, waits for them, and re-layouts, local(): return moved.reshape(count * capacity, 3, steps_total)  11.8 us
    scatter x1, local copies, waits for them, and re-layouts, local(): jnp.zeros((count * capacity, 3 * steps_total), jnp.bfloat16).at[slot]  5.32 us
    reshape x1, local copies, waits for them, and re-layouts, local(): packed.reshape(count, capacity, 3 * steps_total)  4.25 us
  transfers between devices with their start and end apart: 1, of which 1 were waited for; matrix products, arithmetic and copies ran while one was open for 2% of the time, Pallas kernels for 0%

commit v1 on v0

v1 whole, which is shorter than its diff:
```python
import jax
import jax.numpy as jnp
from jax import lax
from jax.sharding import PartitionSpec as P


def slots(route, capacity):
    owner = route[:, 0]
    place = jnp.arange(owner.shape[0], dtype=jnp.int32)
    before = (owner[:, None] == owner[None, :]) & (place[:, None] < place[None, :])
    return owner * capacity + jnp.sum(before.astype(jnp.int32), axis=0)


def local(coeffs, basis, route):
    points = basis.shape[1]
    count = lax.axis_size(("inlet", "row"))
    capacity = 3 * points // (2 * count)
    panel = lax.all_gather(coeffs, "row", axis=1, tiled=True)[0]
    steps = panel.shape[0]
    slot = slots(route, capacity).reshape(1, points)
    onehot = (jnp.arange(count * capacity, dtype=jnp.int32)[:, None] == slot).astype(jnp.float32)
    packed = jnp.einsum("sp,pcm->csm", onehot, basis[0], precision=lax.Precision.HIGHEST)
    packed = packed.reshape(3, count, capacity, -1).transpose(1, 0, 2, 3).reshape(count * 3 * capacity, -1)
    velocity = jnp.einsum("sm,tm->st", packed, panel, precision=lax.Precision.HIGH)
    velocity = velocity.astype(jnp.bfloat16).reshape(count, 3 * capacity, steps)
    moved = lax.all_to_all(velocity, ("inlet", "row"), split_axis=0, concat_axis=0, tiled=True)
    moved = moved.reshape(count, 3, capacity, steps).transpose(0, 2, 1, 3)
    return moved.reshape(count * capacity, 3, steps)


def solution(mesh):
    in_specs = (P("inlet", "row", None), P("inlet", "row", None, None), P(("inlet", "row"), None))
    out_specs = P(("inlet", "row"), None, None)
    return jax.shard_map(local, mesh=mesh, in_specs=in_specs, out_specs=out_specs, check_vma=False)
```

time: 182 us -> 156 us (0.86)
  waiting for transfers between devices: 49.1 us -> 26.4 us
  blocking collectives: 76 us -> 64.6 us
  local copies, waits for them, and re-layouts: 26.8 us -> 33 us
  matrix products: 12.7 us -> 16.1 us
    all_gather x1, waiting for transfers between devices: 48.4 us -> 25.7 us  [local(): panel = lax.all_gather(coeffs, 'row', axis=1, tiled=True)[0]]
    all_to_all x1, blocking collectives: 76 us -> 64.6 us  [local(): lax.all_to_all(velocity, ('inlet', 'row'), split_axis=0, concat_axis=0, t...]
    transpose x0 -> x2, local copies, waits for them, and re-layouts: none -> 9.67 us  [the longest x1 6.68 us: local(): packed.reshape(3, count, capacity, -1).transpose(1, 0, 2, 3)]
    scatter x1 -> x0, local copies, waits for them, and re-layouts: 5.32 us -> none  [local(): jnp.zeros((count * capacity, 3 * steps_total), jnp.bfloat16).at[slot]]
    dot_general x1 -> x2, matrix products: 12.7 us -> 16.1 us  [the longest x1 11.7 us: local(): jnp.einsum('sm,tm->st', packed, panel, precision=lax.Precision.HIGH)]
    reshape x4, local copies, waits for them, and re-layouts: 18.7 us -> 22 us  [the longest x2 13 us: local(): packed.reshape(3, count, capacity, -1).transpose(1, 0, 2, 3)]
    convert_element_type x1 -> x0, local copies, waits for them, and re-layouts: 2.59 us -> none  [local(): velocity = velocity.astype(jnp.bfloat16).reshape(points, 3 * steps_total)]
  transfers between devices with their start and end apart: 1 -> 1, of which waited for: 1 -> 1; matrix products, arithmetic and copies ran while one was open for 2% -> 17% of each run, Pallas kernels for 0% -> 0%
where the time goes in v1:
time: 156 us; the launch traced here: 155 us
  blocking collectives  64.6 us (41%)
  local copies, waits for them, and re-layouts  33 us (21%)
  waiting for transfers between devices  26.4 us (17%)
  matrix products  16.1 us (10%)
  between operations  13.4 us (9%)
  other arithmetic  1.72 us (1%)
    all_to_all x1, blocking collectives, local(): lax.all_to_all(velocity, ('inlet', 'row'), split_axis=0, concat_axis=0, t...  64.6 us
    all_gather x1, waiting for transfers between devices, local(): panel = lax.all_gather(coeffs, 'row', axis=1, tiled=True)[0]  25.7 us
    reshape x2, local copies, waits for them, and re-layouts, local(): packed.reshape(3, count, capacity, -1).transpose(1, 0, 2, 3)  13 us
    dot_general x1, matrix products, local(): jnp.einsum('sm,tm->st', packed, panel, precision=lax.Precision.HIGH)  11.7 us
    transpose x1, local copies, waits for them, and re-layouts, local(): packed.reshape(3, count, capacity, -1).transpose(1, 0, 2, 3)  6.68 us
    reshape x1, local copies, waits for them, and re-layouts, local(): return moved.reshape(count * capacity, 3, steps)  4.91 us
    dot_general x1, matrix products, local(): jnp.einsum('sp,pcm->csm', onehot, basis[0], precision=lax.Precision.HIGHEST)  4.44 us
    reshape x1, local copies, waits for them, and re-layouts, local(): velocity = velocity.astype(jnp.bfloat16).reshape(count, 3 * capacity, steps)  4.07 us
  transfers between devices with their start and end apart: 1, of which 1 were waited for; matrix products, arithmetic and copies ran while one was open for 17% of the time, Pallas kernels for 0%

profile of v1, /device:TPU:0, one launch (start us, length us, event | category | flops | bytes accessed | tf_op | source)
XLA Modules:
  0.0 155.3 jit_solution(6075480435706694023)
XLA Ops:
  6.5 0.0 copy-start
  6.5 0.0 all-gather.2.cloned.1.call-start
  6.5 0.7 all-gather.2.cloned.1.call-update
  7.3 1.0 convert_reduce_fusion
  8.3 0.7 multiply_add_fusion
  9.0 0.0 copy-done
  9.0 4.4 %fusion.7 = f32[3,384,1024]{2,1,0:T(8,128)} fusion(f32[1,256,3,1024]{3,1,2,0:T(8,128)S(1)} %copy-done, s32[256]{0:T(256)S(1)} %multiply_add_fusion), kind=kOutput, calls=%fused_computation.5 | convolution fusion | flops 3623976960 | bytes 7865344 | tf_op jit(solution)/shard_map/sp,pcm->csm/dot_general | solution.py:22
  13.4 6.4 %reshape.25 = f32[3,32,12,1024]{3,2,1,0:T(8,128)} reshape(f32[3,384,1024]{2,1,0:T(8,128)} %fusion.7) | data formatting | bytes 9437184 | tf_op jit(solution)/shard_map/reshape | solution.py:23
  19.8 6.7 %copy.8 = f32[32,3,12,1024]{3,2,1,0:T(8,128)} copy(f32[32,3,12,1024]{3,2,0,1:T(8,128)} %bitcast.23) | data formatting | bytes 9437184 | tf_op jit(solution)/shard_map/transpose | solution.py:23
  26.5 6.6 %reshape.26 = f32[1152,1024]{1,0:T(8,128)} reshape(f32[32,3,12,1024]{3,2,1,0:T(8,128)} %copy.8) | data formatting | bytes 9437184 | tf_op jit(solution)/shard_map/reshape | solution.py:23
  33.1 25.7 %all-gather.2.cloned.1.call-done = f32[1,1024,1024]{2,1,0:T(8,128)} async-done(((f32[1,128,1024]{2,1,0:T(8,128)}), f32[1,1024,1024]{2,1,0:T(8,128)}) %all-gather.2.cloned.1.call-update) | async-done | bytes 4194320 | tf_op jit(solution)/shard_map/all_gather | solution.py:18
  58.8 11.7 %fusion.2 = bf16[1152,1024]{1,0:T(8,128)(2,1)} fusion(f32[1152,1024]{1,0:T(8,128)} %reshape.26, f32[1,1024,1024]{2,1,0:T(8,128)} %all-gather.2.cloned.1.call-done), kind=kOutput, calls=%fused_computation.2 | convolution fusion | flops 7248936960 | bytes 11272192 | tf_op jit(solution)/shard_map/sm,tm->st/dot_general | solution.py:24
  70.5 4.1 %reshape.27 = bf16[32,36,1024]{2,1,0:T(8,128)(2,1)} reshape(bf16[1152,1024]{1,0:T(8,128)(2,1)} %fusion.2) | data formatting | bytes 4718592 | tf_op jit(solution)/shard_map/reshape | solution.py:25
  74.6 64.6 %all_to_all.5 = bf16[32,36,1024]{2,1,0:T(8,128)(2,1)S(1)} all-to-all(bf16[32,36,1024]{2,1,0:T(8,128)(2,1)} %reshape.27), channel_id=1, replica_groups=mesh['inlet'=4,'row'=8] {'inlet','row'}, dimensions={0} | all-to-all | bytes 4718592 | tf_op jit(solution)/shard_map/all_to_all | solution.py:26
  139.2 1.3 copy.9
  140.5 3.0 %copy.10 = bf16[32,12,3,1024]{3,1,0,2:T(8,128)(2,1)} copy(bf16[32,12,3,1024]{3,0,1,2:T(8,128)(2,1)S(1)} %bitcast.24) | data formatting | bytes 4718592 | tf_op jit(solution)/shard_map/transpose | solution.py:27
  143.5 4.9 %reshape.29 = bf16[384,3,1024]{2,0,1:T(8,128)(2,1)} reshape(bf16[32,12,3,1024]{3,1,0,2:T(8,128)(2,1)} %copy.10) | data formatting | bytes 4718592 | tf_op jit(solution)/shard_map/reshape | solution.py:28
Async XLA Ops:
  6.5 2.4 %copy-start = (f32[1,256,3,1024]{3,1,2,0:T(8,128)S(1)}, f32[1,256,3,1024]{3,1,2,0:T(8,128)}, u32[]{:S(2)}) copy-start(f32[1,256,3,1024]{3,1,2,0:T(8,128)} %param.4) | copy-start | bytes 9437188
  6.5 52.3 %all-gather.2.cloned.1.call-start = ((), (), s32[]{:S(2)}) async-start(), calls=%async_computation.1 | async-start | bytes 4718592 | tf_op jit(solution)/shard_map/all_gather | solution.py:18
Sparse Core Ops, SparseCore 0:
  9.0 49.8 all-gather.1

commit v2 on v1

--- a/solution.py
+++ b/solution.py
@@ -1,7 +1,231 @@
 import jax
 import jax.numpy as jnp
+import numpy as np
 from jax import lax
+from jax.experimental import pallas as pl
+from jax.experimental.pallas import tpu as pltpu
 from jax.sharding import PartitionSpec as P
+
+MESH = pl.DeviceIdType.MESH
+CAPACITY, ROWS, REST, WIDE = 12, 32, 4, 256
+F32, BF16 = jnp.float32, jnp.bfloat16
+NT = (((1,), (1,)), ((), ()))
+
+
+def halves(x):
+    high = x.astype(BF16)
+    return high, (x - high.astype(F32)).astype(BF16)
+
+
+def exchange(coeffs, basis, slot, main, rest, panel, base_h, base_l, pack_h, pack_l, pan_h, pan_l, out, rest32, out_rest,
+             g_send, g_recv, own_sem, a_send, a_recv, x_send, x_recv):
+    inlet, row = lax.axis_index("inlet"), lax.axis_index("row")
+    me = inlet * 8 + row
+    z, core = row // 2, row % 2
+
+    def step(kind, zc, src):
+        target = (row + 2, row - 2, z * 2 + 1 - core)[kind]
+        return pltpu.make_async_remote_copy(
+            src_ref=src, dst_ref=panel.at[zc * 2 + core], send_sem=g_send.at[kind, zc],
+            recv_sem=g_recv.at[zc * 2 + core], device_id=(inlet, target), device_id_type=MESH)
+
+    def arrived(chunk):
+        pltpu.make_async_copy(panel.at[chunk], panel.at[chunk], g_recv.at[chunk]).wait()
+
+    def sends(zc):
+        return ((zc <= z) & (z < 3), (zc >= z) & (z > 0))
+
+    @pl.when(z < 3)
+    def _():
+        step(0, z, coeffs).start()
+
+    @pl.when(z > 0)
+    def _():
+        step(1, z, coeffs).start()
+
+    step(2, z, coeffs).start()
+    own = pltpu.make_async_copy(coeffs, panel.at[row], own_sem)
+    own.start()
+
+    @pl.loop(0, 3)
+    def _(c):
+        at = pl.ds(pl.multiple_of(c * 256, 256), 256)
+        high, low = halves(basis[at, :])
+        base_h[at, :] = high
+        base_l[at, :] = low
+
+    points = jnp.broadcast_to(slot[...], (128, 256))
+
+    @pl.loop(0, 9)
+    def _(tile):
+        line = lax.broadcasted_iota(jnp.int32, (128, 256), 0) + tile * 128
+        q = line & 31
+        c = (q >= 12).astype(jnp.int32) + (q >= 24).astype(jnp.int32)
+        key = (line >> 5) * CAPACITY + q - 12 * c
+        tail = line - 32 * ROWS
+        in_tail = tail >= 0
+        key = jnp.where(in_tail, (tail & 31) * CAPACITY + 8 + (tail >> 5), key)
+        c = jnp.where(in_tail, 2, c)
+        hit = key == points
+        pick = jnp.concatenate(
+            [jnp.where(hit & (c == k), 1.0, 0.0).astype(BF16) for k in range(3)], axis=1)
+        at = pl.ds(pl.multiple_of(tile * 128, 128), 128)
+        pack_h[at, :] = jnp.dot(pick, base_h[...], preferred_element_type=F32).astype(BF16)
+        pack_l[at, :] = jnp.dot(pick, base_l[...], preferred_element_type=F32).astype(BF16)
+
+    def product(at):
+        total = lax.dot_general(pack_h[at, :], pan_h[...], NT, preferred_element_type=F32)
+        total += lax.dot_general(pack_l[at, :], pan_h[...], NT, preferred_element_type=F32)
+        return total + lax.dot_general(pack_h[at, :], pan_l[...], NT, preferred_element_type=F32)
+
+    def piece(zc, owner):
+        return pltpu.make_async_remote_copy(
+            src_ref=out.at[zc, owner], dst_ref=main.at[zc, me], send_sem=a_send.at[zc], recv_sem=a_recv.at[zc],
+            device_id=(owner // 8, owner % 8), device_id_type=MESH)
+
+    def last(owner):
+        return pltpu.make_async_remote_copy(
+            src_ref=out_rest.at[owner], dst_ref=rest.at[me], send_sem=x_send, recv_sem=x_recv,
+            device_id=(owner // 8, owner % 8), device_id_type=MESH)
+
+    for k in range(4):
+        near = [(0, 1, 2, 3), (1, 0, 2, 3), (2, 3, 1, 0), (3, 2, 1, 0)]
+        zc = jnp.where(z == 0, near[0][k], jnp.where(z == 1, near[1][k], jnp.where(z == 2, near[2][k], near[3][k])))
+        if k == 0:
+            own.wait()
+        else:
+            arrived(zc * 2 + core)
+            right, left = sends(zc)
+
+            @pl.when(right)
+            def _():
+                step(0, zc, panel.at[zc * 2 + core]).start()
+
+            @pl.when(left)
+            def _():
+                step(1, zc, panel.at[zc * 2 + core]).start()
+
+            step(2, zc, panel.at[zc * 2 + core]).start()
+        arrived(zc * 2 + 1 - core)
+        for part in range(2):
+            high, low = halves(panel[zc * 2 + part])
+            pan_h[part * 128:part * 128 + 128, :] = high
+            pan_l[part * 128:part * 128 + 128, :] = low
+
+        @pl.loop(0, 4)
+        def _(turn):
+            group = (turn + inlet) % 4
+            at = pl.ds(pl.multiple_of(group * 256, 256), 256)
+            out[zc, pl.ds(group * 8, 8)] = product(at).astype(BF16).reshape(8, ROWS, WIDE)
+
+            @pl.loop(0, 8)
+            def _(j):
+                owner = group * 8 + (j + row) % 8
+
+                @pl.when(owner != me)
+                def _():
+                    piece(zc, owner).start()
+
+                @pl.when(owner == me)
+                def _():
+                    pltpu.make_async_copy(out.at[zc, me], main.at[zc, me], a_recv.at[zc]).start()
+
+        tail = product(pl.ds(32 * ROWS, 32 * REST))
+        for e in range(REST):
+            for part in range(2):
+                rest32[pl.ds(e * 8 + zc * 2 + part, 32, stride=32), :] = (
+                    tail[e * 32:e * 32 + 32, part * 128:part * 128 + 128])
+
+    out_rest[...] = rest32[...].astype(BF16).reshape(32, 32, 128)
+
+    @pl.loop(0, 32)
+    def _(j):
+        owner = (j + me) % 32
+
+        @pl.when(owner != me)
+        def _():
+            last(owner).start()
+
+        @pl.when(owner == me)
+        def _():
+            pltpu.make_async_copy(out_rest.at[me], rest.at[me], x_recv).start()
+
+    for zc in range(4):
+        right, left = sends(zc)
+
+        @pl.when(right)
+        def _():
+            step(0, zc, coeffs).wait_send()
+
+        @pl.when(left)
+        def _():
+            step(1, zc, coeffs).wait_send()
+
+        step(2, zc, coeffs).wait_send()
+        some = out.at[zc, pl.ds(0, 31)]
+        pltpu.make_async_copy(some, some, a_send.at[zc]).wait()
+        pltpu.make_async_copy(main.at[zc], main.at[zc], a_recv.at[zc]).wait()
+    some = out_rest.at[pl.ds(0, 31)]
+    pltpu.make_async_copy(some, some, x_send).wait()
+    pltpu.make_async_copy(rest, rest, x_recv).wait()
+
+
+def settle(pick_main, pick_rest, main, rest, inflow):
+    for zc in range(4):
+        at = slice(zc * WIDE, zc * WIDE + WIDE)
+        block = jnp.dot(pick_main[...], main[zc].reshape(4 * ROWS, WIDE), preferred_element_type=F32)
+        block += jnp.dot(pick_rest[...], rest[:, at], preferred_element_type=F32)
+        inflow[:, :, at] = block.astype(BF16).reshape(3, 48, WIDE)
+
+
+def picks():
+    full = np.zeros((144, 4 * 36), np.float32)
+    for c in range(3):
+        for s in range(4):
+            for r in range(CAPACITY):
+                q = c * CAPACITY + r
+                full[c * 48 + s * CAPACITY + r, s * ROWS + q if q < ROWS else 4 * ROWS + s * REST + q - ROWS] = 1
+    return jnp.asarray(full[:, :4 * ROWS], BF16), jnp.asarray(full[:, 4 * ROWS:], BF16)
+
+
+def fused(coeffs, basis, route):
+    slot = slots(route, CAPACITY).reshape(1, 256)
+    rows = basis[0].transpose(1, 0, 2).reshape(768, 1024)
+    vmem = pl.BlockSpec(memory_space=pltpu.VMEM)
+    hbm = pl.BlockSpec(memory_space=pl.ANY)
+    dma = pltpu.SemaphoreType.DMA
+    main, rest = pl.pallas_call(
+        exchange,
+        out_shape=[jax.ShapeDtypeStruct((4, 32, ROWS, WIDE), BF16), jax.ShapeDtypeStruct((32, 32, 128), BF16)],
+        in_specs=[vmem] * 3,
+        out_specs=[hbm] * 2,
+        scratch_shapes=[
+            pltpu.VMEM((8, 128, 1024), F32),
+            pltpu.VMEM((768, 1024), BF16), pltpu.VMEM((768, 1024), BF16),
+            pltpu.VMEM((1152, 1024), BF16), pltpu.VMEM((1152, 1024), BF16),
+            pltpu.VMEM((WIDE, 1024), BF16), pltpu.VMEM((WIDE, 1024), BF16),
+            pltpu.VMEM((4, 32, ROWS, WIDE), BF16),
+            pltpu.VMEM((1024, 128), F32), pltpu.VMEM((32, 32, 128), BF16),
+            dma((3, 4)), dma((8,)), dma, dma((4,)), dma((4,)), dma, dma,
+        ],
+        compiler_params=pltpu.CompilerParams(has_side_effects=True, vmem_limit_bytes=44 << 20),
+        cost_estimate=pl.CostEstimate(flops=10_000_000_000, bytes_accessed=8_000_000, transcendentals=0),
+    )(coeffs[0], rows, slot)
+    pick_main, pick_rest = picks()
+    inflow = pl.pallas_call(
+        settle,
+        grid=(8,),
+        out_shape=jax.ShapeDtypeStruct((3, 384, 1024), BF16),
+        in_specs=[
+            pl.BlockSpec((144, 4 * ROWS), lambda i: (0, 0)),
+            pl.BlockSpec((144, 4 * REST), lambda i: (0, 0)),
+            pl.BlockSpec((4, 4, ROWS, WIDE), lambda i: (0, i, 0, 0)),
+            pl.BlockSpec((4 * REST, 1024), lambda i: (i, 0)),
+        ],
+        out_specs=pl.BlockSpec((3, 48, 1024), lambda i: (0, i, 0)),
+        compiler_params=pltpu.CompilerParams(vmem_limit_bytes=16 << 20),
+    )(pick_main, pick_rest, main, rest.reshape(128, 1024))
+    return inflow.transpose(1, 0, 2)
 
 
 def slots(route, capacity):
@@ -29,6 +253,14 @@
 
 
 def solution(mesh):
+    sizes = dict(mesh.shape)
     in_specs = (P("inlet", "row", None), P("inlet", "row", None, None), P(("inlet", "row"), None))
     out_specs = P(("inlet", "row"), None, None)
-    return jax.shard_map(local, mesh=mesh, in_specs=in_specs, out_specs=out_specs, check_vma=False)
+
+    def body(coeffs, basis, route):
+        shapes = (coeffs.shape, basis.shape, route.shape)
+        if sizes == {"inlet": 4, "row": 8} and shapes == ((1, 128, 1024), (1, 256, 3, 1024), (256, 1)):
+            return fused(coeffs, basis, route)
+        return local(coeffs, basis, route)
+
+    return jax.shard_map(body, mesh=mesh, in_specs=in_specs, out_specs=out_specs, check_vma=False)

time: 156 us -> 102 us (0.65)
  Pallas kernels: 0 us -> 96.8 us
  blocking collectives: 64.6 us -> 0 us
  local copies, waits for them, and re-layouts: 33 us -> 3.05 us
  waiting for transfers between devices: 26.4 us -> 0 us
  matrix products: 16.1 us -> 0 us
  between operations: 13.4 us -> 0.04 us
    pallas_call x0 -> x2, Pallas kernels: none -> 96.8 us  [the longest x1 92.4 us: fused(): pl.pallas_call(exchange, out_shape=[jax.ShapeDtypeStruct((4, 32, ROWS, WI...]
    all_to_all x1 -> x0, blocking collectives: 64.6 us -> none  [local(): lax.all_to_all(velocity, ('inlet', 'row'), split_axis=0, concat_axis=0, t...]
    all_gather x1 -> x0, waiting for transfers between devices: 25.7 us -> none  [local(): panel = lax.all_gather(coeffs, 'row', axis=1, tiled=True)[0]]
    reshape x4 -> x1, local copies, waits for them, and re-layouts: 22 us -> 0.12 us  [fused(): rest.reshape(128, 1024)]
    dot_general x2 -> x0, matrix products: 16.1 us -> none  [the longest x1 11.7 us: local(): jnp.einsum('sm,tm->st', packed, panel, precision=lax.Precision.HIGH)]
    transpose x2 -> x0, local copies, waits for them, and re-layouts: 9.67 us -> none  [the longest x1 6.68 us: local(): packed.reshape(3, count, capacity, -1).transpose(1, 0, 2, 3)]
    unnamed x2 -> x8, local copies, waits for them, and re-layouts: 0.01 us -> 2.94 us
  transfers between devices with their start and end apart: 1 -> 0, of which waited for: 1 -> 0; matrix products, arithmetic and copies ran while one was open for 17% -> 0% of each run, Pallas kernels for 0% -> 0%
where the time goes in v2:
time: 102 us; the launch traced here: 101 us
  Pallas kernels  96.8 us (95%)
  local copies, waits for them, and re-layouts  3.05 us (3%)
  other arithmetic  1.55 us (2%)
    pallas_call x1, Pallas kernels, fused(): pl.pallas_call(exchange, out_shape=[jax.ShapeDtypeStruct((4, 32, ROWS, WI...  92.4 us
    pallas_call x1, Pallas kernels, fused(): pl.pallas_call(settle, grid=(8,), out_shape=jax.ShapeDtypeStruct((3, 384,...  4.43 us
    unnamed x8, local copies, waits for them, and re-layouts  2.94 us

profile of v2, /device:TPU:0, one launch (start us, length us, event | category | flops | bytes accessed | tf_op | source)
XLA Modules:
  0.0 101.4 jit_solution(15437153076824202933)
XLA Ops:
  0.0 0.9 convert_reduce_fusion
  0.9 0.7 bitcast_add_fusion.slot
  1.6 0.0 copy-start.2
  1.6 1.9 %copy-done.2 = f32[1,256,3,1024]{3,1,2,0:T(8,128)S(1)} copy-done((f32[1,256,3,1024]{3,1,2,0:T(8,128)S(1)}, f32[1,256,3,1024]{3,1,2,0:T(8,128)}, u32[]{:S(2)}) %copy-start.2) | copy-done | bytes 3145752
  3.4 0.0 copy-start.3
  3.4 1.0 %copy-done.3 = f32[1,128,1024]{2,1,0:T(8,128)S(1)} copy-done((f32[1,128,1024]{2,1,0:T(8,128)S(1)}, f32[1,128,1024]{2,1,0:T(8,128)}, u32[]{:S(2)}) %copy-start.3) | copy-done | bytes 524312
  4.5 0.0 copy-start
  4.5 0.0 copy-start.1
  4.5 92.4 %shard_map.55 = (bf16[4,32,32,256]{3,2,1,0:T(8,128)(2,1)S(1)}, bf16[32,32,128]{2,1,0:T(8,128)(2,1)S(1)}) custom-call(f32[128,1024]{1,0:T(8,128)S(1)} %bitcast.12, f32[768,1024]{1,0:T(8,128)S(1)} %bitcast.11, s32[1,256]{1,0:T(1,128)S(1)} %bitcast_add_fusion.slot), custom_call_target="tpu_custom_call" | custom-call | flops 10000000000 | bytes 8000000 | tf_op jit(solution)/shard_map/pallas_call | solution.py:197
  96.9 0.1 reshape.28.rest
  97.0 0.0 copy-done
  97.0 0.0 copy-done.1
  97.0 4.4 %shard_map.56 = bf16[3,384,1024]{2,1,0:T(8,128)(2,1)} custom-call(bf16[144,128]{1,0:T(8,128)(2,1)S(1)} %copy-done.1, bf16[144,16]{1,0:T(8,128)(2,1)S(1)} %copy-done, bf16[4,32,32,256]{3,2,1,0:T(8,128)(2,1)S(1)} %get-tuple-element.7.main, bf16[128,1024]{1,0:T(8,128)(2,1)S(1)} %reshape.28.rest), custom_call_target="tpu_custom_call" | custom-call | tf_op jit(solution)/shard_map/pallas_call | solution.py:215
Async XLA Ops:
  1.6 1.9 %copy-start.2 = (f32[1,256,3,1024]{3,1,2,0:T(8,128)S(1)}, f32[1,256,3,1024]{3,1,2,0:T(8,128)}, u32[]{:S(2)}) copy-start(f32[1,256,3,1024]{3,1,2,0:T(8,128)} %param.6) | copy-start | bytes 9437188
  3.4 1.0 %copy-start.3 = (f32[1,128,1024]{2,1,0:T(8,128)S(1)}, f32[1,128,1024]{2,1,0:T(8,128)}, u32[]{:S(2)}) copy-start(f32[1,128,1024]{2,1,0:T(8,128)} %param.5) | copy-start | bytes 1572868
  4.5 92.5 %copy-start = (bf16[144,16]{1,0:T(8,128)(2,1)S(1)}, bf16[144,16]{1,0:T(8,128)(2,1)}, u32[]{:S(2)}) copy-start(bf16[144,16]{1,0:T(8,128)(2,1)} %constant.9.clone.pick_rest) | copy-start | bytes 13828
  4.5 92.5 %copy-start.1 = (bf16[144,128]{1,0:T(8,128)(2,1)S(1)}, bf16[144,128]{1,0:T(8,128)(2,1)}, u32[]{:S(2)}) copy-start(bf16[144,128]{1,0:T(8,128)(2,1)} %constant.8.clone.pick_main) | copy-start | bytes 110596

commit v3 on v2

--- a/solution.py
+++ b/solution.py
@@ -8,6 +8,7 @@
 
 MESH = pl.DeviceIdType.MESH
 CAPACITY, ROWS, REST, WIDE = 12, 32, 4, 256
+SET = 8
 F32, BF16 = jnp.float32, jnp.bfloat16
 NT = (((1,), (1,)), ((), ()))
 
@@ -18,7 +19,7 @@
 
 
 def exchange(coeffs, basis, slot, main, rest, panel, base_h, base_l, pack_h, pack_l, pan_h, pan_l, out, rest32, out_rest,
-             g_send, g_recv, own_sem, a_send, a_recv, x_send, x_recv):
+             b_vmem, b_sem, g_send, g_recv, own_sem, a_send, a_recv, x_send, x_recv):
     inlet, row = lax.axis_index("inlet"), lax.axis_index("row")
     me = inlet * 8 + row
     z, core = row // 2, row % 2
@@ -47,14 +48,24 @@
     own = pltpu.make_async_copy(coeffs, panel.at[row], own_sem)
     own.start()
 
+    fetch = pltpu.make_async_copy(basis, b_vmem, b_sem)
+    fetch.start()
+    fetch.wait()
+
     @pl.loop(0, 3)
     def _(c):
         at = pl.ds(pl.multiple_of(c * 256, 256), 256)
-        high, low = halves(basis[at, :])
+        high, low = halves(b_vmem[at, :])
         base_h[at, :] = high
         base_l[at, :] = low
 
-    points = jnp.broadcast_to(slot[...], (128, 256))
+    owner_of = slot[...]
+    named = lax.broadcasted_iota(jnp.int32, (32, 256), 0) == owner_of
+    named = jnp.where(named, 1.0, 0.0)
+    before = lax.broadcasted_iota(jnp.int32, (256, 256), 0) < lax.broadcasted_iota(jnp.int32, (256, 256), 1)
+    before = jnp.where(before, 1.0, 0.0).astype(BF16)
+    rank = jnp.sum(named * jnp.dot(named.astype(BF16), before, preferred_element_type=F32), axis=0, keepdims=True)
+    points = jnp.broadcast_to(owner_of * CAPACITY + rank.astype(jnp.int32), (128, 256))
 
     @pl.loop(0, 9)
     def _(tile):
@@ -173,23 +184,23 @@
 def settle(pick_main, pick_rest, main, rest, inflow):
     for zc in range(4):
         at = slice(zc * WIDE, zc * WIDE + WIDE)
-        block = jnp.dot(pick_main[...], main[zc].reshape(4 * ROWS, WIDE), preferred_element_type=F32)
+        block = jnp.dot(pick_main[...], main[zc].reshape(SET * ROWS, WIDE), preferred_element_type=F32)
         block += jnp.dot(pick_rest[...], rest[:, at], preferred_element_type=F32)
-        inflow[:, :, at] = block.astype(BF16).reshape(3, 48, WIDE)
+        inflow[:, :, at] = block.astype(BF16).reshape(3, SET * CAPACITY, WIDE)
 
 
 def picks():
-    full = np.zeros((144, 4 * 36), np.float32)
+    full = np.zeros((SET * 36, SET * 36), np.float32)
     for c in range(3):
-        for s in range(4):
+        for s in range(SET):
             for r in range(CAPACITY):
                 q = c * CAPACITY + r
-                full[c * 48 + s * CAPACITY + r, s * ROWS + q if q < ROWS else 4 * ROWS + s * REST + q - ROWS] = 1
-    return jnp.asarray(full[:, :4 * ROWS], BF16), jnp.asarray(full[:, 4 * ROWS:], BF16)
+                full[(c * SET + s) * CAPACITY + r, s * ROWS + q if q < ROWS else SET * ROWS + s * REST + q - ROWS] = 1
+    return jnp.asarray(full[:, :SET * ROWS], BF16), jnp.asarray(full[:, SET * ROWS:], BF16)
 
 
 def fused(coeffs, basis, route):
-    slot = slots(route, CAPACITY).reshape(1, 256)
+    slot = route.reshape(1, 256)
     rows = basis[0].transpose(1, 0, 2).reshape(768, 1024)
     vmem = pl.BlockSpec(memory_space=pltpu.VMEM)
     hbm = pl.BlockSpec(memory_space=pl.ANY)
@@ -197,7 +208,7 @@
     main, rest = pl.pallas_call(
         exchange,
         out_shape=[jax.ShapeDtypeStruct((4, 32, ROWS, WIDE), BF16), jax.ShapeDtypeStruct((32, 32, 128), BF16)],
-        in_specs=[vmem] * 3,
+        in_specs=[hbm, hbm, vmem],
         out_specs=[hbm] * 2,
         scratch_shapes=[
             pltpu.VMEM((8, 128, 1024), F32),
@@ -206,23 +217,24 @@
             pltpu.VMEM((WIDE, 1024), BF16), pltpu.VMEM((WIDE, 1024), BF16),
             pltpu.VMEM((4, 32, ROWS, WIDE), BF16),
             pltpu.VMEM((1024, 128), F32), pltpu.VMEM((32, 32, 128), BF16),
+            pltpu.VMEM((768, 1024), F32), dma,
             dma((3, 4)), dma((8,)), dma, dma((4,)), dma((4,)), dma, dma,
         ],
-        compiler_params=pltpu.CompilerParams(has_side_effects=True, vmem_limit_bytes=44 << 20),
+        compiler_params=pltpu.CompilerParams(has_side_effects=True, vmem_limit_bytes=60 << 20),
         cost_estimate=pl.CostEstimate(flops=10_000_000_000, bytes_accessed=8_000_000, transcendentals=0),
     )(coeffs[0], rows, slot)
     pick_main, pick_rest = picks()
     inflow = pl.pallas_call(
         settle,
-        grid=(8,),
+        grid=(32 // SET,),
         out_shape=jax.ShapeDtypeStruct((3, 384, 1024), BF16),
         in_specs=[
-            pl.BlockSpec((144, 4 * ROWS), lambda i: (0, 0)),
-            pl.BlockSpec((144, 4 * REST), lambda i: (0, 0)),
-            pl.BlockSpec((4, 4, ROWS, WIDE), lambda i: (0, i, 0, 0)),
-            pl.BlockSpec((4 * REST, 1024), lambda i: (i, 0)),
+            pl.BlockSpec((SET * 36, SET * ROWS), lambda i: (0, 0)),
+            pl.BlockSpec((SET * 36, SET * REST), lambda i: (0, 0)),
+            pl.BlockSpec((4, SET, ROWS, WIDE), lambda i: (0, i, 0, 0)),
+            pl.BlockSpec((SET * REST, 1024), lambda i: (i, 0)),
         ],
-        out_specs=pl.BlockSpec((3, 48, 1024), lambda i: (0, i, 0)),
+        out_specs=pl.BlockSpec((3, SET * CAPACITY, 1024), lambda i: (0, i, 0)),
         compiler_params=pltpu.CompilerParams(vmem_limit_bytes=16 << 20),
     )(pick_main, pick_rest, main, rest.reshape(128, 1024))
     return inflow.transpose(1, 0, 2)

time: 102 us -> 99.4 us (0.975)
  other arithmetic: 1.55 us -> 0 us
    unnamed x8 -> x6, local copies, waits for them, and re-layouts: 2.94 us -> 1.59 us
    pallas_call x1, Pallas kernels: 4.43 us -> 3.11 us  [fused(): pl.pallas_call(settle, grid=(32 // SET,), out_shape=jax.ShapeDtypeStruct(...]
where the time goes in v3:
time: 99.4 us; the launch traced here: 99.2 us
  Pallas kernels  96.5 us (97%)
  local copies, waits for them, and re-layouts  2.66 us (3%)
    pallas_call x1, Pallas kernels, fused(): pl.pallas_call(exchange, out_shape=[jax.ShapeDtypeStruct((4, 32, ROWS, WI...  93.4 us
    pallas_call x1, Pallas kernels, fused(): pl.pallas_call(settle, grid=(32 // SET,), out_shape=jax.ShapeDtypeStruct(...  3.11 us

profile of v3, /device:TPU:0, one launch (start us, length us, event | category | flops | bytes accessed | tf_op | source)
XLA Modules:
  0.0 99.2 jit_solution(14657858697935929029)
XLA Ops:
  0.0 0.0 copy-start.1
  0.0 0.0 copy-start.2
  0.0 93.4 %shard_map.55 = (bf16[4,32,32,256]{3,2,1,0:T(8,128)(2,1)}, bf16[32,32,128]{2,1,0:T(8,128)(2,1)}) custom-call(f32[128,1024]{1,0:T(8,128)} %bitcast.9, f32[768,1024]{1,0:T(8,128)} %bitcast.8, s32[1,256]{1,0:T(1,128)} %bitcast.10), custom_call_target="tpu_custom_call" | custom-call | flops 10000000000 | bytes 8000000 | tf_op jit(solution)/shard_map/pallas_call | solution.py:208
  93.4 1.1 %reshape.11.rest = bf16[128,1024]{1,0:T(8,128)(2,1)S(1)} reshape(bf16[32,32,128]{2,1,0:T(8,128)(2,1)} %get-tuple-element.8) | data formatting | bytes 524288 | tf_op jit(solution)/shard_map/reshape | solution.py:239
  94.4 0.0 copy-done.1
  94.5 0.0 copy-done.2
  94.5 0.0 copy-start
  94.5 1.6 %copy-done = bf16[4,32,32,256]{3,2,1,0:T(8,128)(2,1)S(1)} copy-done((bf16[4,32,32,256]{3,2,1,0:T(8,128)(2,1)S(1)}, bf16[4,32,32,256]{3,2,1,0:T(8,128)(2,1)}, u32[]{:S(2)}) %copy-start) | copy-done | bytes 2097176
  96.1 3.1 %shard_map.56 = bf16[3,384,1024]{2,1,0:T(8,128)(2,1)} custom-call(bf16[288,256]{1,0:T(8,128)(2,1)S(1)} %copy-done.1, bf16[288,32]{1,0:T(8,128)(2,1)S(1)} %copy-done.2, bf16[4,32,32,256]{3,2,1,0:T(8,128)(2,1)S(1)} %copy-done, bf16[128,1024]{1,0:T(8,128)(2,1)S(1)} %reshape.11.rest), custom_call_target="tpu_custom_call" | custom-call | tf_op jit(solution)/shard_map/pallas_call | solution.py:227
Async XLA Ops:
  0.0 94.4 %copy-start.1 = (bf16[288,256]{1,0:T(8,128)(2,1)S(1)}, bf16[288,256]{1,0:T(8,128)(2,1)}, u32[]{:S(2)}) copy-start(bf16[288,256]{1,0:T(8,128)(2,1)} %constant.4.clone.pick_main) | copy-start | bytes 442372
  0.0 94.5 %copy-start.2 = (bf16[288,32]{1,0:T(8,128)(2,1)S(1)}, bf16[288,32]{1,0:T(8,128)(2,1)}, u32[]{:S(2)}) copy-start(bf16[288,32]{1,0:T(8,128)(2,1)} %constant.5.clone.pick_rest) | copy-start | bytes 55300
  94.5 1.6 %copy-start = (bf16[4,32,32,256]{3,2,1,0:T(8,128)(2,1)S(1)}, bf16[4,32,32,256]{3,2,1,0:T(8,128)(2,1)}, u32[]{:S(2)}) copy-start(bf16[4,32,32,256]{3,2,1,0:T(8,128)(2,1)} %get-tuple-element.7.main) | copy-start | bytes 6291460

commit v4 on v3

--- a/solution.py
+++ b/solution.py
@@ -24,27 +24,30 @@
     me = inlet * 8 + row
     z, core = row // 2, row % 2
 
-    def step(kind, zc, src):
+    def step(kind, zc, src, half):
         target = (row + 2, row - 2, z * 2 + 1 - core)[kind]
         return pltpu.make_async_remote_copy(
-            src_ref=src, dst_ref=panel.at[zc * 2 + core], send_sem=g_send.at[kind, zc],
-            recv_sem=g_recv.at[zc * 2 + core], device_id=(inlet, target), device_id_type=MESH)
-
-    def arrived(chunk):
-        pltpu.make_async_copy(panel.at[chunk], panel.at[chunk], g_recv.at[chunk]).wait()
+            src_ref=src.at[pl.ds(half * 64, 64)], dst_ref=panel.at[zc * 2 + core, pl.ds(half * 64, 64)],
+            send_sem=g_send.at[kind, zc, half], recv_sem=g_recv.at[zc * 2 + core, half], device_id=(inlet, target), device_id_type=MESH)
+
+    def arrived(chunk, half):
+        block = panel.at[chunk, pl.ds(half * 64, 64)]
+        pltpu.make_async_copy(block, block, g_recv.at[chunk, half]).wait()
 
     def sends(zc):
         return ((zc <= z) & (z < 3), (zc >= z) & (z > 0))
 
-    @pl.when(z < 3)
-    def _():
-        step(0, z, coeffs).start()
-
-    @pl.when(z > 0)
-    def _():
-        step(1, z, coeffs).start()
-
-    step(2, z, coeffs).start()
+    for half in range(2):
+        @pl.when(z < 3)
+        def _():
+            step(0, z, coeffs, half).start()
+
+        @pl.when(z > 0)
+        def _():
+            step(1, z, coeffs, half).start()
+
+        step(2, z, coeffs, half).start()
+
     own = pltpu.make_async_copy(coeffs, panel.at[row], own_sem)
     own.start()
 
@@ -105,19 +108,21 @@
         if k == 0:
             own.wait()
         else:
-            arrived(zc * 2 + core)
-            right, left = sends(zc)
-
-            @pl.when(right)
-            def _():
-                step(0, zc, panel.at[zc * 2 + core]).start()
-
-            @pl.when(left)
-            def _():
-                step(1, zc, panel.at[zc * 2 + core]).start()
-
-            step(2, zc, panel.at[zc * 2 + core]).start()
-        arrived(zc * 2 + 1 - core)
+            for half in range(2):
+                arrived(zc * 2 + core, half)
+                right, left = sends(zc)
+
+                @pl.when(right)
+                def _():
+                    step(0, zc, panel.at[zc * 2 + core], half).start()
+
+                @pl.when(left)
+                def _():
+                    step(1, zc, panel.at[zc * 2 + core], half).start()
+
+                step(2, zc, panel.at[zc * 2 + core], half).start()
+        for half in range(2):
+            arrived(zc * 2 + 1 - core, half)
         for part in range(2):
             high, low = halves(panel[zc * 2 + part])
             pan_h[part * 128:part * 128 + 128, :] = high
@@ -166,13 +171,16 @@
 
         @pl.when(right)
         def _():
-            step(0, zc, coeffs).wait_send()
+            for half in range(2):
+                step(0, zc, coeffs, half).wait_send()
 
         @pl.when(left)
         def _():
-            step(1, zc, coeffs).wait_send()
-
-        step(2, zc, coeffs).wait_send()
+            for half in range(2):
+                step(1, zc, coeffs, half).wait_send()
+
+        for half in range(2):
+            step(2, zc, coeffs, half).wait_send()
         some = out.at[zc, pl.ds(0, 31)]
         pltpu.make_async_copy(some, some, a_send.at[zc]).wait()
         pltpu.make_async_copy(main.at[zc], main.at[zc], a_recv.at[zc]).wait()
@@ -218,7 +226,7 @@
             pltpu.VMEM((4, 32, ROWS, WIDE), BF16),
             pltpu.VMEM((1024, 128), F32), pltpu.VMEM((32, 32, 128), BF16),
             pltpu.VMEM((768, 1024), F32), dma,
-            dma((3, 4)), dma((8,)), dma, dma((4,)), dma((4,)), dma, dma,
+            dma((3, 4, 2)), dma((8, 2)), dma, dma((4,)), dma((4,)), dma, dma,
         ],
         compiler_params=pltpu.CompilerParams(has_side_effects=True, vmem_limit_bytes=60 << 20),
         cost_estimate=pl.CostEstimate(flops=10_000_000_000, bytes_accessed=8_000_000, transcendentals=0),

time: 99.4 us -> 96.6 us (0.972)
  Pallas kernels: 96.5 us -> 93.7 us
    pallas_call x1, Pallas kernels: 93.4 us -> 90.6 us  [fused(): pl.pallas_call(exchange, out_shape=[jax.ShapeDtypeStruct((4, 32, ROWS, WI...]
where the time goes in v4:
time: 96.6 us; the launch traced here: 96.4 us
  Pallas kernels  93.7 us (97%)
  local copies, waits for them, and re-layouts  2.66 us (3%)
    pallas_call x1, Pallas kernels, fused(): pl.pallas_call(exchange, out_shape=[jax.ShapeDtypeStruct((4, 32, ROWS, WI...  90.6 us
    pallas_call x1, Pallas kernels, fused(): pl.pallas_call(settle, grid=(32 // SET,), out_shape=jax.ShapeDtypeStruct(...  3.11 us

profile of v4, /device:TPU:0, one launch (start us, length us, event | category | flops | bytes accessed | tf_op | source)
XLA Modules:
  0.0 96.4 jit_solution(4281458761439608245)
XLA Ops:
  0.0 0.0 copy-start.1
  0.0 0.0 copy-start.2
  0.0 90.6 %shard_map.55 = (bf16[4,32,32,256]{3,2,1,0:T(8,128)(2,1)}, bf16[32,32,128]{2,1,0:T(8,128)(2,1)}) custom-call(f32[128,1024]{1,0:T(8,128)} %bitcast.9, f32[768,1024]{1,0:T(8,128)} %bitcast.8, s32[1,256]{1,0:T(1,128)} %bitcast.10), custom_call_target="tpu_custom_call" | custom-call | flops 10000000000 | bytes 8000000 | tf_op jit(solution)/shard_map/pallas_call | solution.py:216
  90.6 1.1 %reshape.11.rest = bf16[128,1024]{1,0:T(8,128)(2,1)S(1)} reshape(bf16[32,32,128]{2,1,0:T(8,128)(2,1)} %get-tuple-element.8) | data formatting | bytes 524288 | tf_op jit(solution)/shard_map/reshape | solution.py:247
  91.7 0.0 copy-done.1
  91.7 0.0 copy-done.2
  91.7 0.0 copy-start
  91.7 1.6 %copy-done = bf16[4,32,32,256]{3,2,1,0:T(8,128)(2,1)S(1)} copy-done((bf16[4,32,32,256]{3,2,1,0:T(8,128)(2,1)S(1)}, bf16[4,32,32,256]{3,2,1,0:T(8,128)(2,1)}, u32[]{:S(2)}) %copy-start) | copy-done | bytes 2097176
  93.3 3.1 %shard_map.56 = bf16[3,384,1024]{2,1,0:T(8,128)(2,1)} custom-call(bf16[288,256]{1,0:T(8,128)(2,1)S(1)} %copy-done.1, bf16[288,32]{1,0:T(8,128)(2,1)S(1)} %copy-done.2, bf16[4,32,32,256]{3,2,1,0:T(8,128)(2,1)S(1)} %copy-done, bf16[128,1024]{1,0:T(8,128)(2,1)S(1)} %reshape.11.rest), custom_call_target="tpu_custom_call" | custom-call | tf_op jit(solution)/shard_map/pallas_call | solution.py:235
Async XLA Ops:
  0.0 91.7 %copy-start.1 = (bf16[288,256]{1,0:T(8,128)(2,1)S(1)}, bf16[288,256]{1,0:T(8,128)(2,1)}, u32[]{:S(2)}) copy-start(bf16[288,256]{1,0:T(8,128)(2,1)} %constant.4.clone.pick_main) | copy-start | bytes 442372
  0.0 91.7 %copy-start.2 = (bf16[288,32]{1,0:T(8,128)(2,1)S(1)}, bf16[288,32]{1,0:T(8,128)(2,1)}, u32[]{:S(2)}) copy-start(bf16[288,32]{1,0:T(8,128)(2,1)} %constant.5.clone.pick_rest) | copy-start | bytes 55300
  91.7 1.6 %copy-start = (bf16[4,32,32,256]{3,2,1,0:T(8,128)(2,1)S(1)}, bf16[4,32,32,256]{3,2,1,0:T(8,128)(2,1)}, u32[]{:S(2)}) copy-start(bf16[4,32,32,256]{3,2,1,0:T(8,128)(2,1)} %get-tuple-element.7.main) | copy-start | bytes 6291460
